TPU v7x, 32 devices: a whole 2x2x4 slice. The times are simulated.
32 devices in a mesh: ctx: 4 (over z), row: 2 (over y), col: 4 (over x, core).
Axes of the slice: x: 2, y: 2, z: 4, core: 2. Of those that a mesh axis runs over, the one named last changes fastest.
Arguments:
- tokens: bfloat16 [2048, 8192], P(('ctx', 'row'), 'col'), may hold values from -9 to 9
- w_query: bfloat16 [8192, 2048], P('ctx', 'col'), may hold values from -0.0625 to 0.0625
- key_value_weight: bfloat16 [8192, 512], P('ctx', 'col'), may hold values from -0.0625 to 0.0625
- segment: int32 [2048], P(('ctx', 'row')), may hold values from 0 to 7, never falling along the last dimension, each value on 1 to 1024 neighbouring positions
Outputs:
- attended: bfloat16 [2048, 2048], P(('ctx', 'row'), 'col')
Inputs may be any that keep to these rules, and one draw needn't show every extreme that they name: `segment`: document ids never fall along the sequence; a document holds 1 to 1024 tokens.
All inputs are finite; a program needn't handle non-finite values.
Results may differ from a plain program's by a relative error of at most 0.011.
Values may be sent and summed in bfloat16 or wider, within the bound.
A program may use at most 64 MiB of HBM per device.

v0:
```python
import math
import jax
import jax.numpy as jnp
from jax import lax
from jax.sharding import PartitionSpec as P


def swapped(x, axis, stride):
    return lax.ppermute(x, axis, [(i, i ^ 1 << stride) for i in range(lax.axis_size(axis))])


def passed_along(x, axis, by):
    peers = lax.axis_size(axis)
    pairs = [(i, i + by) for i in range(peers) if 0 <= i + by < peers]
    return lax.ppermute(x, axis, pairs)


def local(tokens, w_query, key_value_weight, segment):
    half = tokens.shape[0]
    head_size = key_value_weight.shape[1]
    whole = lax.all_gather(tokens, "col", axis=1, tiled=True)
    query_acc = jnp.dot(
        whole,
        lax.all_gather(w_query, "ctx", axis=0, tiled=True),
        preferred_element_type=jnp.float32,
    )
    keyval_acc = jnp.dot(
        whole,
        lax.all_gather(key_value_weight, "ctx", axis=0, tiled=True),
        preferred_element_type=jnp.float32,
    )
    query = query_acc.astype(jnp.bfloat16)
    mine = keyval_acc.astype(jnp.bfloat16)
    is_even = lax.axis_index("col") % 2 == 0
    partner = swapped(mine, "col", 0)
    joined = jnp.concatenate(
        [jnp.where(is_even, mine, partner), jnp.where(is_even, partner, mine)], axis=1
    )
    block_kv, block_seg = (
        lax.all_gather(joined, "row", axis=0, tiled=True),
        lax.all_gather(segment, "row", axis=0, tiled=True),
    )
    prev_kv, prev_seg = passed_along((block_kv, block_seg), "ctx", 1)
    heads = query.shape[1] // head_size
    queries = query.reshape(half, heads, head_size)
    block = block_kv.shape[0]
    ctx_index = lax.axis_index("ctx")
    query_pos = lax.axis_index("row") * half + jnp.arange(half)
    key_pos = jnp.arange(block)
    own_allow = (key_pos[None, :] <= query_pos[:, None]) & (segment[:, None] == block_seg[None, :])
    prev_allow = (ctx_index > 0) & (segment[:, None] == prev_seg[None, :])
    scale = 1.0 / math.sqrt(head_size)

    def scores(key_value_rows, allow):
        score = (
            jnp.einsum(
                "qhd,kd->hqk",
                queries,
                key_value_rows[:, :head_size],
                preferred_element_type=jnp.float32,
            )
            * scale
        )
        return jnp.where(allow[None], score, -jnp.inf)

    parts = [(scores(block_kv, own_allow), block_kv), (scores(prev_kv, prev_allow), prev_kv)]
    top = parts[0][0].max(axis=-1, keepdims=True)
    for score, key_value_rows in parts[1:]:
        top = jnp.maximum(top, score.max(axis=-1, keepdims=True))
    total = jnp.zeros(top.shape[:2], jnp.float32)
    numer = jnp.zeros((half, heads, head_size), jnp.float32)
    for score, key_value_rows in parts:
        weight = jnp.exp(score - top)
        total = total + jnp.sum(weight, axis=-1)
        probs = weight.astype(jnp.bfloat16)
        numer = numer + jnp.einsum(
            "hqk,kd->qhd", probs, key_value_rows[:, head_size:], preferred_element_type=jnp.float32
        )
    result = (numer / jnp.transpose(total)[:, :, None]).astype(jnp.bfloat16)
    return result.reshape(half, heads * head_size)


def solution(mesh):
    in_specs = (P(("ctx", "row"), "col"), P("ctx", "col"), P("ctx", "col"), P(("ctx", "row")))
    out_specs = P(("ctx", "row"), "col")
    return jax.shard_map(local, mesh=mesh, in_specs=in_specs, out_specs=out_specs, check_vma=False)
```

profile of v0, /device:TPU:0, one launch (start us, length us, event | category | flops | bytes accessed | tf_op | source)
XLA Modules:
  0.0 262.4 jit_solution(787395383971608503)
XLA Ops:
  6.5 0.0 copy-start
  6.5 0.0 all-gather.7.cloned.1.call-start
  6.5 0.7 all-gather.7.cloned.1.call-update
  7.3 0.0 all-gather.5.cloned.1.call-start
  7.3 0.7 all-gather.5.cloned.1.call-update
  8.0 0.0 all-gather.9.cloned.1.call-start
  8.1 0.7 all-gather.9.cloned.1.call-update
  8.7 0.0 copy-done
  8.8 5.2 %all-gather = s32[2,1,256]{2,1,0:T(1,128)S(1)} all-gather(s32[1,1,256]{2,1,0:T(1,128)S(1)} %bitcast.56), channel_id=1, replica_groups=mesh['ctx'=4,'row'=2,'col'=4] {'row'}, dimensions={0}, use_global_device_ids=true | all-gather | bytes 3072 | tf_op jit(solution)/shard_map/all_gather | solution.py:41
  13.9 4.0 %collective-permute-start.1 = (s32[512]{0:T(512)S(1)}, s32[512]{0:T(512)S(1)}, u32[]{:S(2)}, u32[]{:S(2)}) collective-permute-start(s32[512]{0:T(512)S(1)} %bitcast.54), channel_id=1, source_target_pairs={{0,8},{8,16},{16,24},{1,9},{9,17},{17,25},{2,10},{10,18},{18,26},{... | collective-permute-start | bytes 6152 | tf_op jit(solution)/shard_map/ppermute | solution.py:15
  18.0 39.6 %all-gather.7.cloned.1.call-done = bf16[8192,128]{1,0:T(8,128)(2,1)} async-done(((bf16[2048,128]{1,0:T(8,128)(2,1)}), bf16[8192,128]{1,0:T(8,128)(2,1)}) %all-gather.7.cloned.1.call-update) | async-done | bytes 2097168 | tf_op jit(solution)/shard_map/all_gather | solution.py:29
  57.6 34.8 %all-gather.5.cloned.1.call-done = bf16[256,8192]{1,0:T(8,128)(2,1)} async-done(((bf16[256,2048]{1,0:T(8,128)(2,1)}), bf16[256,8192]{1,0:T(8,128)(2,1)}) %all-gather.5.cloned.1.call-update) | async-done | bytes 4194320 | tf_op jit(solution)/shard_map/all_gather | solution.py:21
  92.4 4.4 %convolution_convert_fusion.1 = bf16[256,128]{0,1:T(8,128)(2,1)S(1)} fusion(bf16[256,8192]{1,0:T(8,128)(2,1)} %all-gather.5.cloned.1.call-done, bf16[8192,128]{1,0:T(8,128)(2,1)} %all-gather.7.cloned.1.call-done), kind=kOutput, calls=%fused_computation.15 | convolution fusion | flops 536903680 | bytes 6356992 | tf_op jit(solution)/shard_map/dot_general | solution.py:27
  96.8 0.3 collective-permute-start
  97.1 0.0 collective-permute-done.1
  97.1 0.3 compare_and_fusion
  97.4 0.7 collective-permute-done
  98.1 6.3 %all_gather.17 = bf16[512,256]{0,1:T(8,128)(2,1)S(1)} all-gather(bf16[256,256]{0,1:T(8,128)(2,1)S(1)} %pad_maximum_fusion), channel_id=1, replica_groups=mesh['ctx'=4,'row'=2,'col'=4] {'row'}, dimensions={0}, use_global_device_ids=true | all-gather | bytes 393216 | tf_op jit(solution)/shard_map/all_gather | solution.py:40
  104.5 3.4 %collective-permute-start.2 = (bf16[512,256]{0,1:T(8,128)(2,1)S(1)}, bf16[512,256]{0,1:T(8,128)(2,1)S(1)}, u32[]{:S(2)}, u32[]{:S(2)}) collective-permute-start(bf16[512,256]{0,1:T(8,128)(2,1)S(1)} %all_gather.17), channel_id=1, source_target_pairs={{0,8},{8,16},{16,24},{1,9},{9,17},{17,25},{2,10},{10,18},{18,26},{... | collective-permute-start | bytes 786440 | tf_op jit(solution)/shard_map/ppermute | solution.py:15
  107.9 137.2 %all-gather.9.cloned.1.call-done = bf16[8192,512]{1,0:T(8,128)(2,1)} async-done(((bf16[2048,512]{1,0:T(8,128)(2,1)}), bf16[8192,512]{1,0:T(8,128)(2,1)}) %all-gather.9.cloned.1.call-update) | async-done | bytes 8388624 | tf_op jit(solution)/shard_map/all_gather | solution.py:24
  245.1 7.0 %fusion.8 = bf16[32,4,8,128]{3,2,1,0:T(8,128)(2,1)S(1)} fusion(bf16[256,8192]{1,0:T(8,128)(2,1)} %all-gather.5.cloned.1.call-done, bf16[8192,512]{1,0:T(8,128)(2,1)} %all-gather.9.cloned.1.call-done), kind=kOutput, calls=%fused_computation.14 | convolution fusion | flops 2147614720 | bytes 12845056 | tf_op jit(solution)/shard_map/dot_general | solution.py:22
  252.1 0.5 fusion.25
  252.6 0.0 collective-permute-done.2
  252.6 0.5 fusion.4
  253.1 0.5 fusion.10
  253.6 0.7 fusion.2
  254.3 0.7 fusion.7
  255.0 0.8 copy.18
  (5 shorter events, 0.0 us)
Async XLA Ops:
  6.5 2.2 copy-start
  6.5 51.1 %all-gather.7.cloned.1.call-start = ((), (), s32[]{:S(2)}) async-start(), calls=%async_computation.1 | async-start | bytes 2621440 | tf_op jit(solution)/shard_map/all_gather | solution.py:29
  7.3 85.1 %all-gather.5.cloned.1.call-start = ((), (), s32[]{:S(2)}) async-start(), calls=%async_computation | async-start | bytes 5242880 | tf_op jit(solution)/shard_map/all_gather | solution.py:21
  8.0 237.1 %all-gather.9.cloned.1.call-start = ((), (), s32[]{:S(2)}) async-start(), calls=%async_computation.2 | async-start | bytes 10485760 | tf_op jit(solution)/shard_map/all_gather | solution.py:24
  13.9 83.2 %collective-permute-start.1 = (s32[512]{0:T(512)S(1)}, s32[512]{0:T(512)S(1)}, u32[]{:S(2)}, u32[]{:S(2)}) collective-permute-start(s32[512]{0:T(512)S(1)} %bitcast.54), channel_id=1, source_target_pairs={{0,8},{8,16},{16,24},{1,9},{9,17},{17,25},{2,10},{10,18},{18,26},{... | collective-permute-start | bytes 6152 | tf_op jit(solution)/shard_map/ppermute | solution.py:15
  96.8 1.3 collective-permute-start
  104.5 148.1 %collective-permute-start.2 = (bf16[512,256]{0,1:T(8,128)(2,1)S(1)}, bf16[512,256]{0,1:T(8,128)(2,1)S(1)}, u32[]{:S(2)}, u32[]{:S(2)}) collective-permute-start(bf16[512,256]{0,1:T(8,128)(2,1)S(1)} %all_gather.17), channel_id=1, source_target_pairs={{0,8},{8,16},{16,24},{1,9},{9,17},{17,25},{2,10},{10,18},{18,26},{... | collective-permute-start | bytes 786440 | tf_op jit(solution)/shard_map/ppermute | solution.py:15
Sparse Core Ops, SparseCore 0:
  8.9 48.6 all-gather.6
  59.2 33.1 all-gather.4
  94.0 151.0 all-gather.8
where the time goes:
time: 263 us; the launch traced here: 262 us
  waiting for transfers between devices  214 us (81%)
  matrix products  13.6 us (5%)
  between operations  13.2 us (5%)
  blocking collectives  11.5 us (4%)
  starting transfers between devices  7.78 us (3%)
    all_gather x1, waiting for transfers between devices, local(): lax.all_gather(w_query, 'ctx', axis=0, tiled=True)  137 us
    all_gather x1, waiting for transfers between devices, local(): lax.all_gather(key_value_weight, 'ctx', axis=0, tiled=True)  39.6 us
    all_gather x1, waiting for transfers between devices, local(): whole = lax.all_gather(tokens, 'col', axis=1, tiled=True)  34.8 us
    ppermute x2, starting transfers between devices, passed_along(): return lax.ppermute(x, axis, pairs)  7.39 us
    dot_general x1, matrix products, local(): jnp.dot(whole, lax.all_gather(w_query, 'ctx', axis=0, tiled=True), prefer...  6.98 us
    all_gather x1, blocking collectives, local(): lax.all_gather(joined, 'row', axis=0, tiled=True)  6.33 us
  transfers between devices with their start and end apart: 6, of which 4 were waited for; matrix products, arithmetic and copies ran while one was open for 5% of the time, Pallas kernels for 0%

commit v1 on v0

--- a/solution.py
+++ b/solution.py
@@ -3,6 +3,28 @@
 import jax.numpy as jnp
 from jax import lax
 from jax.sharding import PartitionSpec as P
+
+
+def joined_along(tiles, dim):
+    lengths = list(tiles.shape[1:])
+    lengths[dim] *= tiles.shape[0]
+    return jnp.moveaxis(tiles, 0, dim).reshape(lengths)
+
+
+def gather_around(x, axis, dim):
+    size = lax.axis_size(axis)
+    pairs = [(i, (i + 1) % size) for i in range(size)]
+    back = [(b, a) for a, b in pairs]
+    lower, upper = ([], [])
+    for step in range(size - 1):
+        if step % 2 == 0:
+            lower.append(lax.ppermute(lower[-1] if lower else x, axis, pairs))
+        else:
+            upper.append(lax.ppermute(upper[-1] if upper else x, axis, back))
+    blocks = jnp.stack([*lower[::-1], x, *upper])
+    shift = lax.axis_index(axis) - len(lower)
+    blocks = blocks[(jnp.arange(size) - shift) % size]
+    return joined_along(blocks, dim)
 
 
 def swapped(x, axis, stride):
@@ -19,11 +41,7 @@
     half = tokens.shape[0]
     head_size = key_value_weight.shape[1]
     whole = lax.all_gather(tokens, "col", axis=1, tiled=True)
-    query_acc = jnp.dot(
-        whole,
-        lax.all_gather(w_query, "ctx", axis=0, tiled=True),
-        preferred_element_type=jnp.float32,
-    )
+    query_acc = jnp.dot(whole, gather_around(w_query, "ctx", 0), preferred_element_type=jnp.float32)
     keyval_acc = jnp.dot(
         whole,
         lax.all_gather(key_value_weight, "ctx", axis=0, tiled=True),

time: 263 us -> 243 us (0.924)
  waiting for transfers between devices: 214 us -> 124 us
  starting transfers between devices: 7.78 us -> 54.1 us
  local copies, waits for them, and re-layouts: 0.85 us -> 14.3 us
  other arithmetic: 1.05 us -> 12.8 us
    all_gather x1 -> x0, waiting for transfers between devices: 137 us -> none  [local(): lax.all_gather(w_query, 'ctx', axis=0, tiled=True)]
    ppermute x0 -> x3, waiting for transfers between devices: none -> 82.3 us  [the longest x2 82.3 us: gather_around(): lower.append(lax.ppermute(lower[-1] if lower else x, axis, pairs))]
    ppermute x2, waiting for transfers between devices: 0.01 us -> 40.4 us  [passed_along(): return lax.ppermute(x, axis, pairs)]
    all_gather x1, waiting for transfers between devices: 39.6 us -> 0.01 us  [local(): lax.all_gather(key_value_weight, 'ctx', axis=0, tiled=True)]
    all_gather x1, waiting for transfers between devices: 34.8 us -> 0.01 us  [local(): whole = lax.all_gather(tokens, 'col', axis=1, tiled=True)]
    ppermute x2, starting transfers between devices: 7.39 us -> 33.7 us  [passed_along(): return lax.ppermute(x, axis, pairs)]
    ppermute x0 -> x3, starting transfers between devices: none -> 20.3 us  [the longest x2 18.2 us: gather_around(): lower.append(lax.ppermute(lower[-1] if lower else x, axis, pairs))]
    gather x0 -> x3, local copies, waits for them, and re-layouts: none -> 13.4 us  [gather_around(): blocks = blocks[(jnp.arange(size) - shift) % size]]
  transfers between devices with their start and end apart: 6 -> 8, of which waited for: 4 -> 4; matrix products, arithmetic and copies ran while one was open for 5% -> 13% of each run, Pallas kernels for 0% -> 0%
where the time goes in v1:
time: 243 us; the launch traced here: 242 us
  waiting for transfers between devices  124 us (51%)
  starting transfers between devices  54.1 us (22%)
  local copies, waits for them, and re-layouts  14.3 us (6%)
  between operations  13.6 us (6%)
  other arithmetic  12.8 us (5%)
  matrix products  12.5 us (5%)
  blocking collectives  11 us (5%)
    ppermute x2, waiting for transfers between devices, gather_around(): lower.append(lax.ppermute(lower[-1] if lower else x, axis, pairs))  82.3 us
    ppermute x2, waiting for transfers between devices, passed_along(): return lax.ppermute(x, axis, pairs)  40.4 us
    ppermute x2, starting transfers between devices, passed_along(): return lax.ppermute(x, axis, pairs)  33.7 us
    ppermute x2, starting transfers between devices, gather_around(): lower.append(lax.ppermute(lower[-1] if lower else x, axis, pairs))  18.2 us
    gather x3, local copies, waits for them, and re-layouts, gather_around(): blocks = blocks[(jnp.arange(size) - shift) % size]  13.4 us
    unnamed x1, other arithmetic  7.24 us
    all_gather x1, blocking collectives, local(): lax.all_gather(joined, 'row', axis=0, tiled=True)  6.56 us
    dot_general x1, matrix products, local(): jnp.dot(whole, gather_around(w_query, 'ctx', 0), preferred_element_type=j...  5.75 us
  transfers between devices with their start and end apart: 8, of which 4 were waited for; matrix products, arithmetic and copies ran while one was open for 13% of the time, Pallas kernels for 0%

profile of v1, /device:TPU:0, one launch (start us, length us, event | category | flops | bytes accessed | tf_op | source)
XLA Modules:
  0.0 242.3 jit_solution(15312077262738752954)
XLA Ops:
  6.5 0.0 all-gather.6.cloned.1.call-start
  6.5 0.7 all-gather.6.cloned.1.call-update
  7.3 0.0 all-gather.4.cloned.1.call-start
  7.3 0.7 all-gather.4.cloned.1.call-update
  8.0 3.1 %collective-permute-start.1 = (bf16[2048,512]{1,0:T(8,128)(2,1)}, bf16[2048,512]{1,0:T(8,128)(2,1)S(1)}, u32[]{:S(2)}, u32[]{:S(2)}) collective-permute-start(bf16[2048,512]{1,0:T(8,128)(2,1)} %param.5), channel_id=1, source_target_pairs={{0,8},{8,16},{16,24},{24,0},{1,9},{9,17},{17,25},{25,1},{2,10},{10... | collective-permute-start | bytes 6291464 | tf_op jit(solution)/shard_map/ppermute | solution.py:21
  11.1 2.1 collective-permute-start.3
  13.2 80.4 %collective-permute-done.1 = bf16[2048,512]{1,0:T(8,128)(2,1)S(1)} collective-permute-done((bf16[2048,512]{1,0:T(8,128)(2,1)}, bf16[2048,512]{1,0:T(8,128)(2,1)S(1)}, u32[]{:S(2)}, u32[]{:S(2)}) %collective-permute-start.1) | collective-permute-done | bytes 2097184 | tf_op jit(solution)/shard_map/ppermute | solution.py:21
  93.5 15.1 %collective-permute-start.2 = (bf16[2048,512]{1,0:T(8,128)(2,1)S(1)}, bf16[2048,512]{1,0:T(8,128)(2,1)}, u32[]{:S(2)}, u32[]{:S(2)}) collective-permute-start(bf16[2048,512]{1,0:T(8,128)(2,1)S(1)} %collective-permute-done.1), channel_id=1, source_target_pairs={{0,8},{8,16},{16,24},{24,0},{1,9},{9,17},{17,25},{25,1},{2,10},{10... | collective-permute-start | bytes 6291464 | tf_op jit(solution)/shard_map/ppermute | solution.py:21
  108.6 4.4 %all-gather = s32[2,1,256]{2,1,0:T(1,128)S(1)} all-gather(s32[1,1,256]{2,1,0:T(1,128)} %bitcast.62), channel_id=1, replica_groups=mesh['ctx'=4,'row'=2,'col'=4] {'row'}, dimensions={0}, use_global_device_ids=true | all-gather | bytes 3072 | tf_op jit(solution)/shard_map/all_gather | solution.py:59
  113.1 31.1 %collective-permute-start.4 = (s32[512]{0:T(512)S(1)}, s32[512]{0:T(512)S(1)}, u32[]{:S(2)}, u32[]{:S(2)}) collective-permute-start(s32[512]{0:T(512)S(1)} %bitcast.60), channel_id=1, source_target_pairs={{0,8},{8,16},{16,24},{1,9},{9,17},{17,25},{2,10},{10,18},{18,26},{... | collective-permute-start | bytes 6152 | tf_op jit(solution)/shard_map/ppermute | solution.py:37
  144.3 35.5 %collective-permute-done.4 = s32[512]{0:T(512)S(1)} collective-permute-done((s32[512]{0:T(512)S(1)}, s32[512]{0:T(512)S(1)}, u32[]{:S(2)}, u32[]{:S(2)}) %collective-permute-start.4) | collective-permute-done | bytes 2080 | tf_op jit(solution)/shard_map/ppermute | solution.py:37
  179.8 0.9 compare_and_fusion
  180.8 0.0 collective-permute-done.3
  180.8 1.9 collective-permute-done.2
  182.7 3.8 %pad_maximum_fusion = bf16[4,2048,512]{2,1,0:T(8,128)(2,1)S(1)} fusion(bf16[1,2048,512]{2,1,0:T(8,128)(2,1)} %bitcast.7, bf16[1,2048,512]{2,1,0:T(8,128)(2,1)} %bitcast.55, bf16[1,2048,512]{2,1,0:T(8,128)(2,1)S(1)} %bitcast.56, bf16[1,2048,512]{2,1,0:T(8,128)(2,1)} %bitcast.4), kind=kLoop, calls=%fused_computation.2 | loop fusion | flops 12582912 | bytes 16777216 | tf_op jit(solution)/shard_map/stack | solution.py:24
  186.5 3.5 %fusion.22 = (bf16[4,1024,512]{2,1,0:T(8,128)(2,1)}, bf16[4,1024,512]{2,1,0:T(8,128)(2,1)}) fusion(bf16[4,2048,512]{2,1,0:T(8,128)(2,1)S(1)} %pad_maximum_fusion), kind=kLoop, calls=%fused_computation.47 | loop fusion | bytes 16777216 | tf_op jit(solution)/shard_map/gather | solution.py:26
  190.1 4.9 %gather_fusion.1 = bf16[4,1024,512]{2,1,0:T(8,128)(2,1)} fusion(bf16[4,1024,512]{2,1,0:T(8,128)(2,1)} %get-tuple-element.8, s32[1024]{0:T(1024)S(1)} %pad_clamp_fusion), kind=kCustom, calls=%fused_computation.1 | custom fusion | bytes 8388624 | tf_op jit(solution)/shard_map/gather | solution.py:26
  195.0 4.9 %gather_fusion = bf16[4,1024,512]{2,1,0:T(8,128)(2,1)} fusion(bf16[4,1024,512]{2,1,0:T(8,128)(2,1)} %get-tuple-element.7, s32[1024]{0:T(1024)S(1)} %pad_clamp_fusion), kind=kCustom, calls=%fused_computation | custom fusion | bytes 8388624 | tf_op jit(solution)/shard_map/gather | solution.py:26
  199.9 7.2 %pad_maximum_fusion.1 = bf16[4,2048,512]{2,1,0:T(8,128)(2,1)} fusion(bf16[4,1024,512]{2,1,0:T(8,128)(2,1)} %gather_fusion.1, bf16[4,1024,512]{2,1,0:T(8,128)(2,1)} %gather_fusion), kind=kLoop, calls=%fused_computation.3 | loop fusion | flops 16777216 | bytes 16777216
  207.2 4.5 %convolution_convert_fusion.1 = bf16[256,128]{0,1:T(8,128)(2,1)S(1)} fusion(bf16[256,8192]{1,0:T(8,128)(2,1)} %all-gather.4.cloned.1.call-done, bf16[8192,128]{1,0:T(8,128)(2,1)} %all-gather.6.cloned.1.call-done), kind=kOutput, calls=%fused_computation.18 | convolution fusion | flops 536903680 | bytes 6356992 | tf_op jit(solution)/shard_map/dot_general | solution.py:45
  211.7 0.1 collective-permute-start
  211.8 5.7 %convolution_convert_fusion = bf16[512,256]{1,0:T(8,128)(2,1)S(1)} fusion(bf16[8192,512]{1,0:T(8,128)(2,1)} %bitcast.54, bf16[256,8192]{1,0:T(8,128)(2,1)S(1)} %copy-done), kind=kOutput, calls=%fused_computation.17 | convolution fusion | flops 2147614720 | bytes 12845056 | tf_op jit(solution)/shard_map/dot_general | solution.py:44
  217.6 0.0 collective-permute-done
  217.6 6.6 %all_gather.14 = bf16[512,256]{0,1:T(8,128)(2,1)S(1)} all-gather(bf16[256,256]{0,1:T(8,128)(2,1)S(1)} %pad_maximum_fusion.2), channel_id=1, replica_groups=mesh['ctx'=4,'row'=2,'col'=4] {'row'}, dimensions={0}, use_global_device_ids=true | all-gather | bytes 393216 | tf_op jit(solution)/shard_map/all_gather | solution.py:58
  224.2 2.6 %collective-permute-start.5 = (bf16[512,256]{0,1:T(8,128)(2,1)S(1)}, bf16[512,256]{0,1:T(8,128)(2,1)S(1)}, u32[]{:S(2)}, u32[]{:S(2)}) collective-permute-start(bf16[512,256]{0,1:T(8,128)(2,1)S(1)} %all_gather.14), channel_id=1, source_target_pairs={{0,8},{8,16},{16,24},{1,9},{9,17},{17,25},{2,10},{10,18},{18,26},{... | collective-permute-start | bytes 786440 | tf_op jit(solution)/shard_map/ppermute | solution.py:37
  226.8 0.5 fusion.23
  227.3 4.9 %collective-permute-done.5 = bf16[512,256]{0,1:T(8,128)(2,1)S(1)} collective-permute-done((bf16[512,256]{0,1:T(8,128)(2,1)S(1)}, bf16[512,256]{0,1:T(8,128)(2,1)S(1)}, u32[]{:S(2)}, u32[]{:S(2)}) %collective-permute-start.5) | collective-permute-done | bytes 262176 | tf_op jit(solution)/shard_map/ppermute | solution.py:37
  232.2 0.5 fusion.4
  232.7 0.5 fusion.9
  233.2 0.7 fusion.2
  233.9 0.7 fusion.7
  234.6 0.8 copy.18
  (11 shorter events, 0.1 us)
Async XLA Ops:
  6.5 200.7 %all-gather.6.cloned.1.call-start = ((), (), s32[]{:S(2)}) async-start(), calls=%async_computation.1 | async-start | bytes 2621440 | tf_op jit(solution)/shard_map/all_gather | solution.py:47
  7.3 199.9 %all-gather.4.cloned.1.call-start = ((), (), s32[]{:S(2)}) async-start(), calls=%async_computation | async-start | bytes 5242880 | tf_op jit(solution)/shard_map/all_gather | solution.py:43
  8.0 85.5 %collective-permute-start.1 = (bf16[2048,512]{1,0:T(8,128)(2,1)}, bf16[2048,512]{1,0:T(8,128)(2,1)S(1)}, u32[]{:S(2)}, u32[]{:S(2)}) collective-permute-start(bf16[2048,512]{1,0:T(8,128)(2,1)} %param.5), channel_id=1, source_target_pairs={{0,8},{8,16},{16,24},{24,0},{1,9},{9,17},{17,25},{25,1},{2,10},{10... | collective-permute-start | bytes 6291464 | tf_op jit(solution)/shard_map/ppermute | solution.py:21
  11.1 169.7 %collective-permute-start.3 = (bf16[2048,512]{1,0:T(8,128)(2,1)}, bf16[2048,512]{1,0:T(8,128)(2,1)}, u32[]{:S(2)}, u32[]{:S(2)}) collective-permute-start(bf16[2048,512]{1,0:T(8,128)(2,1)} %param.5), channel_id=1, source_target_pairs={{8,0},{16,8},{24,16},{0,24},{9,1},{17,9},{25,17},{1,25},{10,2},{18... | collective-permute-start | bytes 6291464 | tf_op jit(solution)/shard_map/ppermute | solution.py:23
  93.5 89.2 %collective-permute-start.2 = (bf16[2048,512]{1,0:T(8,128)(2,1)S(1)}, bf16[2048,512]{1,0:T(8,128)(2,1)}, u32[]{:S(2)}, u32[]{:S(2)}) collective-permute-start(bf16[2048,512]{1,0:T(8,128)(2,1)S(1)} %collective-permute-done.1), channel_id=1, source_target_pairs={{0,8},{8,16},{16,24},{24,0},{1,9},{9,17},{17,25},{25,1},{2,10},{10... | collective-permute-start | bytes 6291464 | tf_op jit(solution)/shard_map/ppermute | solution.py:21
  113.1 66.7 %collective-permute-start.4 = (s32[512]{0:T(512)S(1)}, s32[512]{0:T(512)S(1)}, u32[]{:S(2)}, u32[]{:S(2)}) collective-permute-start(s32[512]{0:T(512)S(1)} %bitcast.60), channel_id=1, source_target_pairs={{0,8},{8,16},{16,24},{1,9},{9,17},{17,25},{2,10},{10,18},{18,26},{... | collective-permute-start | bytes 6152 | tf_op jit(solution)/shard_map/ppermute | solution.py:37
  207.2 4.6 %copy-start = (bf16[256,8192]{1,0:T(8,128)(2,1)S(1)}, bf16[256,8192]{1,0:T(8,128)(2,1)}, u32[]{:S(2)}) copy-start(bf16[256,8192]{1,0:T(8,128)(2,1)} %all-gather.4.cloned.1.call-done) | copy-start | bytes 12582916
  211.7 5.8 %collective-permute-start = (bf16[256,128]{0,1:T(8,128)(2,1)S(1)}, bf16[256,128]{0,1:T(8,128)(2,1)S(1)}, u32[]{:S(2)}, u32[]{:S(2)}) collective-permute-start(bf16[256,128]{0,1:T(8,128)(2,1)S(1)} %convolution_convert_fusion.1), channel_id=1, source_target_pairs={{0,1},{1,0},{2,3},{3,2},{4,5},{5,4},{6,7},{7,6},{8,9},{9,8},{10,11... | collective-permute-start | bytes 196616 | tf_op jit(solution)/shard_map/ppermute | solution.py:31
  224.2 8.0 %collective-permute-start.5 = (bf16[512,256]{0,1:T(8,128)(2,1)S(1)}, bf16[512,256]{0,1:T(8,128)(2,1)S(1)}, u32[]{:S(2)}, u32[]{:S(2)}) collective-permute-start(bf16[512,256]{0,1:T(8,128)(2,1)S(1)} %all_gather.14), channel_id=1, source_target_pairs={{0,8},{8,16},{16,24},{1,9},{9,17},{17,25},{2,10},{10,18},{18,26},{... | collective-permute-start | bytes 786440 | tf_op jit(solution)/shard_map/ppermute | solution.py:37
Sparse Core Ops, SparseCore 0:
  8.9 101.0 all-gather.5
  111.6 32.6 all-gather.3
